TPU v7x, 256 devices: a whole 4x4x8 slice. The times are simulated.
256 devices in a mesh: island: 8 (over z_hi, core), fsdp: 32 (over x, y, z_lo).
Axes of the slice: x: 4, y: 4, z: 8 (z_hi: 4, z_lo: 2; z = z_hi * 2 + z_lo), core: 2. Of those that a mesh axis runs over, the one named last changes fastest.
Arguments:
- gate_pre: bfloat16 [8, 16384, 512], P('island', 'fsdp'), may hold values from -6 to 6
- up_val: bfloat16 [8, 16384, 512], P('island', 'fsdp'), may hold values from -6 to 6
- out_grad: bfloat16 [8, 16384, 8192], P('island', 'fsdp'), may hold values from -0.625 to 0.625
- inner_weights: float32 [8, 512, 8192], P('island', 'fsdp'), as said below
- first_moment: float32 [8, 512, 8192], P('island', 'fsdp'), may hold values from -4 to 4
- second_moment: float32 [8, 512, 8192], P('island', 'fsdp'), may hold values from 0.01 to 1
- anchor: float32 [512, 8192], P('fsdp'), may hold values from -0.5 to 0.5
- outer_momentum: float32 [512, 8192], P('fsdp', 'island'), may hold values from -1.5 to 1.5
Outputs:
- first_next: float32 [8, 512, 8192], P('island', 'fsdp')
- second_next: float32 [8, 512, 8192], P('island', 'fsdp')
- momentum_next: float32 [512, 8192], P('fsdp', 'island')
- anchor_next: float32 [512, 8192], P('fsdp')
Inputs may be any that keep to these rules, and one draw needn't show every extreme that they name: `inner_weights`: each replica's weights differ from anchor by at most 0.125 in every entry.
All inputs are finite; a program needn't handle non-finite values.
Results may differ from a plain program's by a relative error of at most 0.0042.
Values sent between devices are 32-bit elements; how exact they have to be, the bound alone decides.
A program may use at most 128 MiB of HBM per device.

v0:
```python
import jax
import jax.numpy as jnp
from jax import lax
from jax.sharding import PartitionSpec as P

STEP = 100


def rounded_term(left, right):
    product = lax.dot_general(
        left, right, (((0,), (0,)), ((), ())), preferred_element_type=jnp.float32
    )
    return lax.optimization_barrier(product.astype(jnp.bfloat16)).astype(jnp.float32)


def on_device(
    gate_pre, up_val, out_grad, inner_weights, first_moment, second_moment, anchor, outer_momentum
):
    hidden = (jax.nn.silu(gate_pre[0].astype(jnp.float32)) * up_val[0].astype(jnp.float32)).astype(
        jnp.bfloat16
    )
    cotangent = out_grad[0]
    full_term = rounded_term(hidden, cotangent)
    gradient = lax.psum_scatter(full_term, "fsdp", scatter_dimension=0, tiled=True)
    first_next = 0.9 * first_moment[0] + 0.1 * gradient
    second_next = 0.95 * second_moment[0] + 0.05 * gradient * gradient
    first_fix = 1.0 - 0.9**STEP
    second_fix = 1.0 - 0.95**STEP
    update = first_next / first_fix / (jnp.sqrt(second_next / second_fix) + 1e-08)
    weights_old = inner_weights[0]
    weights_next = weights_old - 0.05 * (update + 0.4 * weights_old)
    departure = anchor - weights_next
    out_cols = outer_momentum.shape[1]
    islands = lax.axis_size("island")
    whole_momentum = lax.all_gather(outer_momentum, "island", axis=1, tiled=True)
    pseudo = lax.psum(departure, "island") / islands
    momentum_full = 0.9 * whole_momentum + pseudo
    anchor_next = anchor - 0.7 * (pseudo + 0.9 * momentum_full)
    momentum_next = lax.dynamic_slice_in_dim(
        momentum_full, lax.axis_index("island") * out_cols, out_cols, 1
    )
    return (first_next[None], second_next[None], momentum_next, anchor_next)


def solution(mesh):
    return jax.shard_map(
        on_device,
        mesh=mesh,
        in_specs=(
            P("island", "fsdp", None),
            P("island", "fsdp", None),
            P("island", "fsdp", None),
            P("island", "fsdp", None),
            P("island", "fsdp", None),
            P("island", "fsdp", None),
            P("fsdp", None),
            P("fsdp", "island"),
        ),
        out_specs=(
            P("island", "fsdp", None),
            P("island", "fsdp", None),
            P("fsdp", "island"),
            P("fsdp", None),
        ),
        check_vma=False,
    )
```

profile of v0, /device:TPU:1, one launch (start us, length us, event | category | flops | bytes accessed | tf_op | source)
XLA Modules:
  0.0 483.3 jit_solution(13340137392930888152)
XLA Ops:
  7.2 0.0 reduce-scatter.2.cloned.1.call-start
  7.2 11.6 %convolution_convert_fusion = bf16[512,8192]{1,0:T(8,128)(2,1)} fusion(bf16[1,512,8192]{2,1,0:T(8,128)(2,1)} %param.10, bf16[1,512,512]{2,1,0:T(8,128)(2,1)} %param.9, bf16[1,512,512]{2,1,0:T(8,128)(2,1)} %param.8), kind=kOutput, calls=%fused_computation | convolution fusion | flops 4301258752 | bytes 17825792 | tf_op jit(solution)/shard_map/dot_general | solution.py:10
  18.8 11.3 %convert_element_type.25 = f32[512,8192]{1,0:T(8,128)} convert(bf16[512,8192]{1,0:T(8,128)(2,1)} %convolution_convert_fusion) | non-fusion elementwise | flops 4194304 | bytes 25165824 | tf_op jit(solution)/shard_map/convert_element_type | solution.py:13
  30.1 0.0 copy-start
  30.1 0.0 copy-start.1
  30.1 0.0 copy-start.2
  30.1 0.0 copy-start.3
  30.2 0.0 copy-start.4
  30.2 0.0 reduce-scatter.2.cloned.1.call-update
  30.2 0.0 all-reduce.2.cloned.1.call-start
  30.2 369.4 %reduce-scatter.2.cloned.1.call-done = f32[16,8192]{1,0:T(8,128)} async-done(((f32[512,8192]{1,0:T(8,128)}), f32[16,8192]{1,0:T(8,128)}) %reduce-scatter.2.cloned.1.call-update) | async-done | bytes 524304 | tf_op jit(solution)/shard_map/reduce_scatter | solution.py:24
  399.6 0.0 copy-done
  399.6 0.0 copy-done.1
  399.6 0.0 copy-done.2
  399.6 0.0 copy-done.3
  399.6 2.4 fusion.9
  402.1 0.0 all-reduce.2.cloned.1.call-update
  402.1 0.0 copy-done.4
  402.1 17.5 %all_gather.3 = f32[16,8192]{1,0:T(8,128)S(1)} all-gather(f32[16,1024]{1,0:T(8,128)S(1)} %copy-done.4), channel_id=1, replica_groups=mesh['island'=8,'fsdp'=32] {'island'}, dimensions={1}, use_global_device_ids=true | all-gather | bytes 589824 | tf_op jit(solution)/shard_map/all_gather | solution.py:35
  419.6 54.2 %all-reduce.2.cloned.1.call-done = f32[16,8192]{1,0:T(8,128)} async-done(((f32[16,8192]{1,0:T(8,128)}), f32[16,8192]{1,0:T(8,128)}) %all-reduce.2.cloned.1.call-update) | async-done | bytes 524304 | tf_op jit(solution)/shard_map/psum | solution.py:36
  473.8 2.0 multiply_subtract_fusion
  475.8 0.6 constant_dynamic-slice_fusion
Async XLA Ops:
  7.2 392.4 %reduce-scatter.2.cloned.1.call-start = ((), (), s32[]{:S(2)}) async-start(), calls=%async_computation.1 | async-start | bytes 17301504 | tf_op jit(solution)/shard_map/reduce_scatter | solution.py:24
  30.1 369.5 %copy-start = (f32[16,8192]{1,0:T(8,128)S(1)}, f32[16,8192]{1,0:T(8,128)}, u32[]{:S(2)}) copy-start(f32[16,8192]{1,0:T(8,128)} %param.14) | copy-start | bytes 1572868
  30.1 369.5 %copy-start.1 = (f32[1,16,8192]{2,1,0:T(8,128)S(1)}, f32[1,16,8192]{2,1,0:T(8,128)}, u32[]{:S(2)}) copy-start(f32[1,16,8192]{2,1,0:T(8,128)} %param.11) | copy-start | bytes 1572868
  30.1 369.5 %copy-start.2 = (f32[1,16,8192]{2,1,0:T(8,128)S(1)}, f32[1,16,8192]{2,1,0:T(8,128)}, u32[]{:S(2)}) copy-start(f32[1,16,8192]{2,1,0:T(8,128)} %param.12) | copy-start | bytes 1572868
  30.1 369.5 %copy-start.3 = (f32[1,16,8192]{2,1,0:T(8,128)S(1)}, f32[1,16,8192]{2,1,0:T(8,128)}, u32[]{:S(2)}) copy-start(f32[1,16,8192]{2,1,0:T(8,128)} %param.13) | copy-start | bytes 1572868
  30.2 371.9 %copy-start.4 = (f32[16,1024]{1,0:T(8,128)S(1)}, f32[16,1024]{1,0:T(8,128)}, u32[]{:S(2)}) copy-start(f32[16,1024]{1,0:T(8,128)} %param.15) | copy-start | bytes 196612
  30.2 443.6 %all-reduce.2.cloned.1.call-start = ((), (), s32[]{:S(2)}) async-start(), calls=%async_computation.2 | async-start | bytes 1048576 | tf_op jit(solution)/shard_map/psum | solution.py:36
Sparse Core Ops, SparseCore 0:
  30.3 369.2 reduce-scatter.1
  402.8 70.9 all-reduce.1
where the time goes:
time: 484 us; the launch traced here: 483 us
  waiting for transfers between devices  424 us (88%)
  blocking collectives  17.5 us (4%)
  other arithmetic  15.7 us (3%)
  between operations  14.1 us (3%)
  matrix products  11.6 us (2%)
    reduce_scatter x1, waiting for transfers between devices, on_device(): lax.psum_scatter(full_term, 'fsdp', scatter_dimension=0, tiled=True)  369 us
    psum x1, waiting for transfers between devices, on_device(): pseudo = lax.psum(departure, 'island') / islands  54.2 us
    all_gather x1, blocking collectives, on_device(): lax.all_gather(outer_momentum, 'island', axis=1, tiled=True)  17.5 us
    dot_general x1, matrix products, rounded_term(): lax.dot_general(left, right, (((0,), (0,)), ((), ())), preferred_element_...  11.6 us
    convert_element_type x1, other arithmetic, rounded_term(): lax.optimization_barrier(product.astype(jnp.bfloat16)).astype(jnp.float32)  11.3 us
  transfers between devices with their start and end apart: 2, of which 2 were waited for; matrix products, arithmetic and copies ran while one was open for 0% of the time, Pallas kernels for 0%

commit v1 on v0

v1 whole, which is shorter than its diff:
```python
import functools

import jax
import jax.numpy as jnp
from jax import lax
from jax.experimental import pallas as pl
from jax.experimental.pallas import tpu as pltpu
from jax.sharding import PartitionSpec as P

MESH = pl.DeviceIdType.MESH
STEP = 100
F32 = jnp.float32
W = 1024
ORDER = [
    (0, 0), (0, 6), (0, 1), (0, 7), (1, 0), (1, 6), (0, 2), (0, 8), (0, 12), (1, 1), (1, 7), (2, 0), (0, 14), (2, 6),
    (0, 3), (1, 2), (1, 8), (1, 12), (2, 1), (3, 6), (2, 7), (3, 0), (0, 13), (1, 3), (0, 9), (2, 8), (3, 1), (4, 0),
    (2, 2), (1, 9), (1, 14), (2, 12), (4, 6), (4, 1), (3, 7), (3, 2), (0, 15), (2, 3), (2, 9), (0, 4), (3, 8), (2, 14),
    (0, 10), (3, 12), (4, 7), (4, 2), (0, 5), (3, 9), (3, 3), (5, 0), (1, 13), (5, 6), (0, 11), (5, 1), (3, 14), (1, 4),
    (1, 10), (6, 0), (4, 8), (4, 12), (4, 3), (1, 5), (1, 11), (4, 9), (1, 15), (5, 7), (2, 13), (5, 2), (4, 14), (5, 8),
    (6, 3), (5, 3), (7, 0), (2, 10), (5, 9), (5, 12), (2, 4), (6, 1), (6, 4), (2, 11), (7, 3), (2, 15), (2, 5), (3, 13),
    (7, 1), (5, 14), (3, 4), (7, 4), (3, 10), (3, 11), (3, 15), (3, 5), (4, 10), (4, 13), (4, 11), (4, 15), (4, 4), (4, 5),
    (5, 10), (5, 13), (5, 11), (5, 15), (5, 4), (5, 5), (6, 6), (6, 5), (6, 7), (6, 2), (7, 6), (7, 5), (7, 7), (7, 2),
]
PER = 13
ISL = 11
N_SEM = 16 * PER + 8 * ISL


def kernel(
    gate, up, og, iw, fm, sm, an, om, fn_o, sn_o, mn_o, an_o,
    gv, uv, ov, iwv, fmv, smv, anv, omv, fnv, snv, mnv, antv,
    hf, hb, T, L1, S1, L2, S2, LZ, CZ, CL1, CS1, CL2, CS2, dep, depc, hz,
    ssem, rsem, lsem, osem,
):
    isl = lax.axis_index("island")
    f = lax.axis_index("fsdp")
    zh, core = isl // 2, isl % 2
    x, y, z = f // 8, (f // 2) % 4, f % 2

    def dev(x, y, z):
        return (isl, (x * 4 + y) * 2 + z)

    xp, xm = dev((x + 1) % 4, y, z), dev((x + 3) % 4, y, z)
    yp, ym = dev(x, (y + 1) % 4, z), dev(x, (y + 3) % 4, z)
    zz = dev(x, y, 1 - z)

    def island(rc, rz):
        return ((zh + rz) % 4) * 2 + (core + rc) % 2

    others = [(1, 0), (0, 1), (0, 2), (0, 3), (1, 1), (1, 2), (1, 3)]

    first = [pltpu.make_async_copy(gate.at[0], gv, lsem.at[0]), pltpu.make_async_copy(up.at[0], uv, lsem.at[1])]
    for c in first:
        c.start()

    def load_unit(u):
        def body(j, _):
            pltpu.make_async_copy(
                og.at[0, :, pl.ds(pl.multiple_of(j * 1024 + u * 128, 128), 128)],
                ov.at[u, :, pl.ds(pl.multiple_of(j * 128, 128), 128)],
                lsem.at[7 + u],
            ).start()
            return 0

        lax.fori_loop(0, 8, body, 0)

    used = []
    for s, i in ORDER:
        if s == 0 and i // 2 not in used:
            used.append(i // 2)
    for u in used:
        load_unit(u)
    state = [
        pltpu.make_async_copy(src, dst, lsem.at[2 + i])
        for i, (src, dst) in enumerate([(iw.at[0], iwv), (fm.at[0], fmv), (sm.at[0], smv), (an, anv), (om, omv)])
    ]
    for c in state:
        c.start()

    barrier = pltpu.get_barrier_semaphore()
    peers = [xp, xm, yp, ym, zz] + [(island(rc, rz), f) for rc, rz in others]
    for d in peers:
        pl.semaphore_signal(barrier, inc=1, device_id=d, device_id_type=MESH)

    for c in first:
        c.wait()

    def silu_rows(t, _):
        rows = pl.ds(pl.multiple_of(t * 128, 128), 128)
        v = gv[rows, :].astype(F32)
        h = v / (1.0 + jnp.exp(-v)) * uv[rows, :].astype(F32)
        hf[:, rows] = h.astype(jnp.bfloat16).astype(F32).T
        return 0

    for t in range(4):
        silu_rows(t, 0)

    def permute(i, _):
        h, kx, ky = i // 16, (i // 4) % 4, i % 4
        base = (((x + kx) % 4) * 4 + (y + ky) % 4) * 2
        a = hf[pl.ds(pl.multiple_of((base + z) * 16 + 8 * h, 8), 8), :]
        b = hf[pl.ds(pl.multiple_of((base + 1 - z) * 16 + 8 * h, 8), 8), :]
        hb[pl.ds(pl.multiple_of(i * 16, 16), 16), :] = jnp.concatenate([a, b], axis=0).astype(jnp.bfloat16)
        return 0

    lax.fori_loop(0, 32, permute, 0)
    pl.semaphore_wait(barrier, len(peers))

    copies = {}

    def send(key, n, src, dst, to):
        c = pltpu.make_async_remote_copy(
            src_ref=src, dst_ref=dst, send_sem=ssem.at[n], recv_sem=rsem.at[n], device_id=to, device_id_type=MESH
        )
        c.start()
        copies[key] = c

    def arrived(*keys):
        for key in keys:
            copies[key].wait_recv()

    def add(dst, *srcs):
        n = dst.shape[0]
        if len(dst.shape) == 2:
            dst[...] = sum([s[...] for s in srcs], dst[...])
            return

        def body(i, _):
            dst[i] = sum([s[i] for s in srcs], dst[i])
            return 0

        lax.fori_loop(0, n, body, 0)

    def matmul(c):
        u, h = c // 2, c % 2

        def body(t, _):
            cols = pl.ds(pl.multiple_of(t * 256, 256), 256)
            r = lax.dot_general(
                hb[256 * h : 256 * h + 256, :], ov[u, :, cols], (((1,), (0,)), ((), ())), preferred_element_type=F32
            )
            T[c, :, :, :, :, cols] = r.astype(jnp.bfloat16).astype(F32).reshape(4, 4, 2, 8, 256)
            return 0

        lax.fori_loop(0, W // 256, body, 0)

    def ring_raw(c, p, blk, one, two, plus, minus):
        base = c * PER + (0 if p == 1 else 6)
        send((c, p, 0), base, blk(2, 0), one(0), plus)
        send((c, p, 1), base + 1, blk(2, 1), one(1), minus)
        send((c, p, 2), base + 2, blk(1, 1), two(0, 1), plus)
        send((c, p, 3), base + 3, blk(3, 0), two(1, 0), minus)

    def ring_mid(c, p, blk, one, two, plus, minus):
        base = c * PER + (0 if p == 1 else 6)
        arrived((c, p, 0))
        add(blk(1, 0), one(0))
        send((c, p, 4), base + 4, blk(1, 0), two(0, 0), plus)
        arrived((c, p, 1))
        add(blk(3, 1), one(1))
        send((c, p, 5), base + 5, blk(3, 1), two(1, 1), minus)

    def ring_end(c, p, blk, one, two, plus, minus):
        arrived(*[(c, p, i) for i in (2, 3, 4, 5)])
        add(blk(0), two(0), two(1))

    def rings(c):
        t = T.at[c]
        two = pl.ds(0, 2), pl.ds(2, 2)
        if c < 12:
            if c < 6:
                b1 = lambda k, half=None: t.at[k] if half is None else t.at[k, two[half]]
                b2 = lambda k, half=None: t.at[0, k] if half is None else t.at[0, k, half]
            else:
                b1 = lambda k, half=None: t.at[:, k] if half is None else t.at[two[half], k]
                b2 = lambda k, half=None: t.at[k, 0] if half is None else t.at[k, 0, half]
            l1 = lambda d, half=None: L1.at[c, d] if half is None else L1.at[c, d, two[half]]
            l2 = lambda d, half=None: L2.at[c, d] if half is None else L2.at[c, d, half]
            s1, s2 = (lambda d: S1.at[c, d]), (lambda d: S2.at[c, d])
        else:
            i = c - 12
            part = pl.ds(0, 512), pl.ds(512, 512)
            if c < 14:
                b1 = lambda k, half=None: t.at[k, :, 0] if half is None else t.at[k, two[half], 0]
                b2 = lambda k, half=None: t.at[0, k, 0] if half is None else t.at[0, k, 0, :, part[half]]
            else:
                b1 = lambda k, half=None: t.at[:, k, 0] if half is None else t.at[two[half], k, 0]
                b2 = lambda k, half=None: t.at[k, 0, 0] if half is None else t.at[k, 0, 0, :, part[half]]
            l1 = lambda d, half=None: CL1.at[i, d] if half is None else CL1.at[i, d, two[half]]
            l2 = lambda d, half=None: CL2.at[i, d] if half is None else CL2.at[i, d, :, part[half]]
            s1, s2 = (lambda d: CS1.at[i, d]), (lambda d: CS2.at[i, d])
        along_x, along_y = (xp, xm), (yp, ym)
        d1, d2 = (along_x, along_y) if c < 6 or 12 <= c < 14 else (along_y, along_x)
        return (c, 1, b1, s1, l1) + d1, (c, 2, b2, s2, l2) + d2

    def update(c):
        u, h = c // 2, c % 2
        rows = pl.ds(8 * h, 8)
        first_fix = 1.0 - 0.9**STEP
        second_fix = 1.0 - 0.95**STEP

        def body(r, _):
            rc, rz = r // 4, r % 4
            j = island(rc, rz)
            cols = pl.ds(pl.multiple_of(j * 1024 + u * 128, 128), 128)
            g = T[c, 0, 0, 0, :, pl.ds(pl.multiple_of(j * 128, 128), 128)]
            first_next = 0.9 * fmv[rows, cols] + 0.1 * g
            second_next = 0.95 * smv[rows, cols] + 0.05 * g * g
            fnv[rows, cols] = first_next
            snv[rows, cols] = second_next
            upd = first_next / first_fix / (jnp.sqrt(second_next / second_fix) + 1e-08)
            w = iwv[rows, cols]
            dep[u, rc, rz, rows, :] = anv[rows, cols] - (w - 0.05 * (upd + 0.4 * w))
            return 0

        lax.fori_loop(0, 8, body, 0)

    updated = [0]
    out_copies = []

    def finish_chunk(c):
        u = c // 2
        if updated[0] == 0:
            for s in state:
                s.wait()
        update(c)
        updated[0] += 1
        done[c] = True
        if done.get(c ^ 1):
            send((u, "core"), 16 * PER + u * ISL, dep.at[u, 1], depc.at[u], (island(1, 0), f))
        if updated[0] == 16:
            for k, (src, dst) in enumerate([(fnv, fn_o.at[0]), (snv, sn_o.at[0])]):
                o = pltpu.make_async_copy(src, dst, osem.at[k])
                o.start()
                out_copies.append(o)

    done = {}
    own = isl * 1024

    def island_one(u):
        arrived((u, "core"))
        add(dep.at[u, 0], depc.at[u])
        for rz in (2, 1, 3):
            send((u, "sum", rz), 16 * PER + u * ISL + rz, dep.at[u, 0, rz], hz.at[u, rz - 1], (island(0, rz), f))

    def island_two(u):
        arrived(*[(u, "sum", rz) for rz in (1, 2, 3)])
        cols = pl.ds(128 * u, 128)
        pseudo = (dep[u, 0, 0] + hz[u, 0] + hz[u, 1] + hz[u, 2]) / 8
        momentum = 0.9 * omv[:, cols] + pseudo
        mnv[:, cols] = momentum
        out = pl.ds(pl.multiple_of(own + u * 128, 128), 128)
        antv[u] = anv[:, out] - 0.7 * (pseudo + 0.9 * momentum)
        for k, (rc, rz) in enumerate([(0, 2), (1, 2), (0, 1), (1, 1), (0, 3), (1, 3), (1, 0)]):
            send((u, "all", k), 16 * PER + u * ISL + 4 + k, antv.at[u], an_o.at[:, out], (island(rc, rz), f))
        o = pltpu.make_async_copy(antv.at[u], an_o.at[:, out], osem.at[3 + u])
        o.start()
        out_copies.append(o)

    for s, i in ORDER:
        if s == 6:
            island_one(i)
            continue
        if s == 7:
            island_two(i)
            continue
        r1, r2 = rings(i)
        if s == 0:
            if i // 2 in used:
                u = i // 2
                used.remove(u)
                pltpu.make_async_copy(og.at[0, :, pl.ds(0, W)], ov.at[u], lsem.at[7 + u]).wait()
            matmul(i)
        if i < 12:
            if s == 0:
                ring_raw(*r1)
            elif s == 1:
                ring_mid(*r1)
            elif s == 2:
                ring_end(*r1)
                ring_raw(*r2)
            elif s == 3:
                ring_mid(*r2)
            elif s == 4:
                ring_end(*r2)
                send((i, "z"), i * PER + 12, T.at[i, 0, 0, 1], LZ.at[i], zz)
            else:
                arrived((i, "z"))
                add(T.at[i, 0, 0, 0], LZ.at[i])
                finish_chunk(i)
        else:
            if s == 0:
                send((i, "z"), i * PER + 12, T.at[i, :, :, 1], CZ.at[i - 12], zz)
            elif s == 1:
                arrived((i, "z"))
                for k in range(4):
                    add(T.at[i, k, :, 0], CZ.at[i - 12, k])
                ring_raw(*r1)
            elif s == 2:
                ring_mid(*r1)
            elif s == 3:
                ring_end(*r1)
                ring_raw(*r2)
            elif s == 4:
                ring_mid(*r2)
            else:
                ring_end(*r2)
                finish_chunk(i)

    o = pltpu.make_async_copy(mnv, mn_o, osem.at[2])
    o.start()
    out_copies.append(o)
    for key, c in copies.items():
        if key[1] == "all":
            c.wait_recv()
    for c in copies.values():
        c.wait_send()
    for o in out_copies:
        o.wait()


def on_device(*args):
    V = pltpu.VMEM
    anyspace = pl.BlockSpec(memory_space=pl.ANY)
    return pl.pallas_call(
        kernel,
        out_shape=(
            jax.ShapeDtypeStruct((1, 16, 8192), F32),
            jax.ShapeDtypeStruct((1, 16, 8192), F32),
            jax.ShapeDtypeStruct((16, 1024), F32),
            jax.ShapeDtypeStruct((16, 8192), F32),
        ),
        in_specs=[anyspace] * 8,
        out_specs=[anyspace] * 4,
        scratch_shapes=[
            V((512, 512), jnp.bfloat16), V((512, 512), jnp.bfloat16), V((8, 512, W), jnp.bfloat16),
            V((16, 8192), F32), V((16, 8192), F32), V((16, 8192), F32), V((16, 8192), F32), V((16, 1024), F32),
            V((16, 8192), F32), V((16, 8192), F32), V((16, 1024), F32), V((8, 16, 128), F32),
            V((512, 512), F32), V((512, 512), jnp.bfloat16), V((16, 4, 4, 2, 8, W), F32),
            V((12, 2, 4, 2, 8, W), F32), V((12, 2, 2, 2, 8, W), F32), V((12, 2, 2, 8, W), F32), V((12, 2, 8, W), F32),
            V((12, 8, W), F32),
            V((4, 4, 4, 8, W), F32), V((4, 2, 4, 8, W), F32), V((4, 2, 2, 8, W), F32), V((4, 2, 8, W), F32),
            V((4, 2, 8, W // 2), F32),
            V((8, 2, 4, 16, 128), F32), V((8, 4, 16, 128), F32), V((8, 3, 16, 128), F32),
            pltpu.SemaphoreType.DMA((N_SEM,)), pltpu.SemaphoreType.DMA((N_SEM,)),
            pltpu.SemaphoreType.DMA((15,)), pltpu.SemaphoreType.DMA((11,)),
        ],
        compiler_params=pltpu.CompilerParams(
            collective_id=0, has_side_effects=True, vmem_limit_bytes=60 * 2**20
        ),
        cost_estimate=pl.CostEstimate(flops=4300000000, bytes_accessed=13000000, transcendentals=400000),
        name="round",
    )(*args)


def solution(mesh):
    rows = P("island", "fsdp", None)
    return jax.shard_map(
        on_device,
        mesh=mesh,
        in_specs=(rows,) * 6 + (P("fsdp", None), P("fsdp", "island")),
        out_specs=(rows, rows, P("fsdp", "island"), P("fsdp", None)),
        check_vma=False,
    )
```

time: 484 us -> 120 us (0.25)
  waiting for transfers between devices: 424 us -> 0 us
  Pallas kernels: 0 us -> 112 us
  blocking collectives: 17.5 us -> 0 us
  other arithmetic: 15.7 us -> 0 us
  between operations: 14.1 us -> 0.64 us
  matrix products: 11.6 us -> 0 us
  local copies, waits for them, and re-layouts: 0.65 us -> 7.08 us
    reduce_scatter x1 -> x0, waiting for transfers between devices: 369 us -> none  [on_device(): lax.psum_scatter(full_term, 'fsdp', scatter_dimension=0, tiled=True)]
    pallas_call x0 -> x1, Pallas kernels: none -> 112 us  [on_device(): pl.pallas_call(kernel, out_shape=(jax.ShapeDtypeStruct((1, 16, 8192), F32...]
    psum x1 -> x0, waiting for transfers between devices: 54.2 us -> none  [on_device(): pseudo = lax.psum(departure, 'island') / islands]
    all_gather x1 -> x0, blocking collectives: 17.5 us -> none  [on_device(): lax.all_gather(outer_momentum, 'island', axis=1, tiled=True)]
    dot_general x1 -> x0, matrix products: 11.6 us -> none  [rounded_term(): lax.dot_general(left, right, (((0,), (0,)), ((), ())), preferred_element_...]
    convert_element_type x1 -> x0, other arithmetic: 11.3 us -> none  [rounded_term(): lax.optimization_barrier(product.astype(jnp.bfloat16)).astype(jnp.float32)]
    unnamed x10 -> x4, local copies, waits for them, and re-layouts: 0.02 us -> 7.08 us
  transfers between devices with their start and end apart: 2 -> 0, of which waited for: 2 -> 0; matrix products, arithmetic and copies ran while one was open for 0% -> 0% of each run, Pallas kernels for 0% -> 0%
where the time goes in v1:
time: 120 us
  Pallas kernels  112 us (93%)
  local copies, waits for them, and re-layouts  7.08 us (6%)
    pallas_call x1, Pallas kernels, on_device(): pl.pallas_call(kernel, out_shape=(jax.ShapeDtypeStruct((1, 16, 8192), F32...  112 us
    unnamed x4, local copies, waits for them, and re-layouts  7.08 us

profile of v1, /device:TPU:1, one launch (start us, length us, event | category | flops | bytes accessed | tf_op | source)
XLA Modules:
  0.0 119.8 jit_solution(10412639146970506816)
XLA Ops:
  0.6 112.1 %round.1 = (f32[1,16,8192]{2,1,0:T(8,128)}, f32[1,16,8192]{2,1,0:T(8,128)}, f32[16,1024]{1,0:T(8,128)}, f32[16,8192]{1,0:T(8,128)}) custom-call(bf16[1,512,512]{2,1,0:T(8,128)(2,1)} %gate.1, bf16[1,512,512]{2,1,0:T(8,128)(2,1)} %up.1, bf16[1,512,8192]{2,1,0:T(8,128)(2,1)} %og.1, f32[1,16,8192]{2,1,0:T(8,128)} %iw.1, f32[1,16,8192]{2,1,0:T(8,128)} %fm.1, ...), custom_call_target="tpu_custom_call" | custom-call | flops 4300000256 | bytes 13000000 | tf_op jit(solution)/shard_map/round/pallas_call | solution.py:325
  112.7 1.9 %copy.16 = f32[1,16,8192]{2,1,0:T(8,128)} copy(f32[1,16,8192]{2,1,0:T(8,128)} %get-tuple-element.8) | data formatting | bytes 1048576
  114.6 1.9 %copy.17 = f32[1,16,8192]{2,1,0:T(8,128)} copy(f32[1,16,8192]{2,1,0:T(8,128)} %get-tuple-element.9) | data formatting | bytes 1048576
  116.5 1.5 %copy.18 = f32[16,1024]{1,0:T(8,128)} copy(f32[16,1024]{1,0:T(8,128)} %get-tuple-element.10) | data formatting | bytes 131072
  117.9 1.9 %copy.19 = f32[16,8192]{1,0:T(8,128)} copy(f32[16,8192]{1,0:T(8,128)} %get-tuple-element.11) | data formatting | bytes 1048576

commit v2 on v1

v2 whole, which is shorter than its diff:
```python
import functools

import jax
import jax.numpy as jnp
from jax import lax
from jax.experimental import pallas as pl
from jax.experimental.pallas import tpu as pltpu
from jax.sharding import PartitionSpec as P

MESH = pl.DeviceIdType.MESH
STEP = 100
F32 = jnp.float32
W = 1024
ORDER = [
    (0, 0), (0, 6), (0, 1), (0, 7), (1, 0), (1, 6), (0, 2), (0, 8), (0, 12), (1, 1), (1, 7), (2, 0), (0, 14), (2, 6),
    (0, 3), (1, 2), (1, 8), (1, 12), (2, 1), (3, 6), (2, 7), (3, 0), (0, 13), (1, 3), (0, 9), (2, 8), (3, 1), (4, 0),
    (2, 2), (1, 9), (1, 14), (2, 12), (4, 6), (4, 1), (3, 7), (3, 2), (0, 15), (2, 3), (2, 9), (0, 4), (3, 8), (2, 14),
    (0, 10), (3, 12), (4, 7), (4, 2), (0, 5), (3, 9), (3, 3), (5, 0), (1, 13), (5, 6), (0, 11), (5, 1), (3, 14), (1, 4),
    (1, 10), (6, 0), (4, 8), (4, 12), (4, 3), (1, 5), (1, 11), (4, 9), (1, 15), (5, 7), (2, 13), (5, 2), (4, 14), (5, 8),
    (6, 3), (5, 3), (7, 0), (2, 10), (5, 9), (5, 12), (2, 4), (6, 1), (6, 4), (2, 11), (7, 3), (2, 15), (2, 5), (3, 13),
    (7, 1), (5, 14), (3, 4), (7, 4), (3, 10), (3, 11), (3, 15), (3, 5), (4, 10), (4, 13), (4, 11), (4, 15), (4, 4), (4, 5),
    (5, 10), (5, 13), (5, 11), (5, 15), (5, 4), (5, 5), (6, 6), (6, 5), (6, 7), (6, 2), (7, 6), (7, 5), (7, 7), (7, 2),
]
PER = 5
N_RECV = 16 * PER + 17
CLASSES = 13

def kernel(
    gate, up, og, iw, fm, sm, an, om, fn_o, sn_o, mn_o, an_o,
    gv, uv, ov, iwv, fmv, smv, anv, omv,
    hb, T, L1, S1, L2, S2, LZ, CZ, CL1, CS1, CL2, CS2, dep, depc, hz,
    ssem, rsem, lsem,
):
    isl = lax.axis_index("island")
    f = lax.axis_index("fsdp")
    zh, core = isl // 2, isl % 2
    x, y, z = f // 8, (f // 2) % 4, f % 2

    def dev(x, y, z):
        return (isl, (x * 4 + y) * 2 + z)

    xp, xm = dev((x + 1) % 4, y, z), dev((x + 3) % 4, y, z)
    yp, ym = dev(x, (y + 1) % 4, z), dev(x, (y + 3) % 4, z)
    zz = dev(x, y, 1 - z)

    def island(rc, rz):
        return ((zh + rz) % 4) * 2 + (core + rc) % 2

    others = [(1, 0), (0, 1), (0, 2), (0, 3), (1, 1), (1, 2), (1, 3)]

    first = [pltpu.make_async_copy(gate.at[0], gv, lsem.at[0]), pltpu.make_async_copy(up.at[0], uv, lsem.at[1])]
    for c in first:
        c.start()

    def load_unit(u):
        def body(j, _):
            pltpu.make_async_copy(
                og.at[0, :, pl.ds(pl.multiple_of(j * 1024 + u * 128, 128), 128)],
                ov.at[u, :, pl.ds(pl.multiple_of(j * 128, 128), 128)],
                lsem.at[7 + u],
            ).start()
            return 0

        lax.fori_loop(0, 8, body, 0)

    used = []
    for s, i in ORDER:
        if s == 0 and i // 2 not in used:
            used.append(i // 2)
    for u in used[:2]:
        load_unit(u)
    state = [
        pltpu.make_async_copy(src, dst, lsem.at[2 + i])
        for i, (src, dst) in enumerate([(iw.at[0], iwv), (fm.at[0], fmv), (sm.at[0], smv), (an, anv), (om, omv)])
    ]
    barrier = pltpu.get_barrier_semaphore()
    peers = [xp, xm, yp, ym, zz] + [(island(rc, rz), f) for rc, rz in others]
    for d in peers:
        pl.semaphore_signal(barrier, inc=1, device_id=d, device_id_type=MESH)

    i = lax.broadcasted_iota(jnp.int32, (512, 512), 0)
    src = ((x + i // 64) % 4) * 128 + ((y + i // 16) % 4) * 32 + ((z + i // 8) % 2) * 16 + (i // 256) * 8 + i % 8
    pick = (src == lax.broadcasted_iota(jnp.int32, (512, 512), 1)).astype(F32).astype(jnp.bfloat16)
    for c in first:
        c.wait()

    for t in range(4):
        rows = slice(128 * t, 128 * t + 128)
        v = gv[rows, :].astype(F32)
        h = (v / (1.0 + jnp.exp(-v)) * uv[rows, :].astype(F32)).astype(jnp.bfloat16)
        hb[:, rows] = lax.dot_general(pick, h, (((1,), (1,)), ((), ())), preferred_element_type=F32).astype(jnp.bfloat16)
    pl.semaphore_wait(barrier, len(peers))

    def remote(n, k, src, dst, to):
        return pltpu.make_async_remote_copy(
            src_ref=src, dst_ref=dst, send_sem=ssem.at[k], recv_sem=rsem.at[n], device_id=to, device_id_type=MESH
        )

    def send(n, k, src, dst, to):
        remote(n, k, src, dst, to).start()

    def arrived(n, whole):
        remote(n, 0, whole, whole, zz).wait_recv()

    def add(dst, *srcs):
        n = dst.shape[0]
        if len(dst.shape) == 2:
            dst[...] = sum([s[...] for s in srcs], dst[...])
            return

        def body(i, _):
            dst[i] = sum([s[i] for s in srcs], dst[i])
            return 0

        lax.fori_loop(0, n, body, 0)

    def matmul(c):
        u, h = c // 2, c % 2

        def body(t, _):
            cols = pl.ds(pl.multiple_of(t * 256, 256), 256)
            r = lax.dot_general(
                hb[256 * h : 256 * h + 256, :], ov[u, :, cols], (((1,), (0,)), ((), ())), preferred_element_type=F32
            )
            T[c, :, :, :, :, cols] = r.astype(jnp.bfloat16).astype(F32).reshape(4, 4, 2, 8, 256)
            return 0

        lax.fori_loop(0, W // 256, body, 0)

    def ring_raw(n, k, blk, one, two, ones, twos, plus, minus):
        send(n, k, blk(2, 0), one(0), plus)
        send(n, k, blk(2, 1), one(1), minus)
        send(n + 1, k + 1, blk(1, 1), two(0, 1), plus)
        send(n + 1, k + 1, blk(3, 0), two(1, 0), minus)

    def ring_mid(n, k, blk, one, two, ones, twos, plus, minus):
        arrived(n, ones)
        add(blk(1, 0), one(0))
        send(n + 1, k + 1, blk(1, 0), two(0, 0), plus)
        add(blk(3, 1), one(1))
        send(n + 1, k + 1, blk(3, 1), two(1, 1), minus)

    def ring_end(n, k, blk, one, two, ones, twos, plus, minus):
        arrived(n + 1, twos)
        add(blk(0), two(0), two(1))

    def rings(c):
        t = T.at[c]
        two = pl.ds(0, 2), pl.ds(2, 2)
        if c < 12:
            if c < 6:
                b1 = lambda k, half=None: t.at[k] if half is None else t.at[k, two[half]]
                b2 = lambda k, half=None: t.at[0, k] if half is None else t.at[0, k, half]
            else:
                b1 = lambda k, half=None: t.at[:, k] if half is None else t.at[two[half], k]
                b2 = lambda k, half=None: t.at[k, 0] if half is None else t.at[k, 0, half]
            l1 = lambda d, half=None: L1.at[c, d] if half is None else L1.at[c, d, two[half]]
            l2 = lambda d, half=None: L2.at[c, d] if half is None else L2.at[c, d, half]
            s1, s2 = (lambda d: S1.at[c, d]), (lambda d: S2.at[c, d])
            w1, w2 = (S1.at[c], L1.at[c]), (S2.at[c], L2.at[c])
            k = 0
        else:
            i = c - 12
            part = pl.ds(0, 512), pl.ds(512, 512)
            if c < 14:
                b1 = lambda k, half=None: t.at[k, :, 0] if half is None else t.at[k, two[half], 0]
                b2 = lambda k, half=None: t.at[0, k, 0] if half is None else t.at[0, k, 0, :, part[half]]
            else:
                b1 = lambda k, half=None: t.at[:, k, 0] if half is None else t.at[two[half], k, 0]
                b2 = lambda k, half=None: t.at[k, 0, 0] if half is None else t.at[k, 0, 0, :, part[half]]
            l1 = lambda d, half=None: CL1.at[i, d] if half is None else CL1.at[i, d, two[half]]
            l2 = lambda d, half=None: CL2.at[i, d] if half is None else CL2.at[i, d, :, part[half]]
            s1, s2 = (lambda d: CS1.at[i, d]), (lambda d: CS2.at[i, d])
            w1, w2 = (CS1.at[i], CL1.at[i]), (CS2.at[i], CL2.at[i])
            k = 5
        along_x, along_y = (xp, xm), (yp, ym)
        d1, d2 = (along_x, along_y) if c < 6 or 12 <= c < 14 else (along_y, along_x)
        n = c * PER
        return (n, k, b1, s1, l1) + w1 + d1, (n + 2, k + 2, b2, s2, l2) + w2 + d2

    def update(c):
        u, h = c // 2, c % 2
        rows = pl.ds(8 * h, 8)
        first_fix = 1.0 - 0.9**STEP
        second_fix = 1.0 - 0.95**STEP

        def body(r, _):
            rc, rz = r // 4, r % 4
            j = island(rc, rz)
            cols = pl.ds(pl.multiple_of(j * 1024 + u * 128, 128), 128)
            g = T[c, 0, 0, 0, :, pl.ds(pl.multiple_of(j * 128, 128), 128)]
            first_next = 0.9 * fmv[rows, cols] + 0.1 * g
            second_next = 0.95 * smv[rows, cols] + 0.05 * g * g
            fn_o[0, rows, cols] = first_next
            sn_o[0, rows, cols] = second_next
            upd = first_next / first_fix / (jnp.sqrt(second_next / second_fix) + 1e-08)
            w = iwv[rows, cols]
            dep[u, rc, rz, rows, :] = anv[rows, cols] - (w - 0.05 * (upd + 0.4 * w))
            return 0

        lax.fori_loop(0, 8, body, 0)

    updated = [0]

    def finish_chunk(c):
        u = c // 2
        if updated[0] == 0:
            for s in state:
                s.wait()
        update(c)
        updated[0] += 1
        done[c] = True
        if done.get(c ^ 1):
            send(16 * PER + 2 * u, 10, dep.at[u, 1], depc.at[u], (island(1, 0), f))

    done = {}
    own = isl * 1024

    def island_one(u):
        arrived(16 * PER + 2 * u, depc.at[u])
        add(dep.at[u, 0], depc.at[u])
        for rz in (2, 1, 3):
            send(16 * PER + 2 * u + 1, 11, dep.at[u, 0, rz], hz.at[u, rz - 1], (island(0, rz), f))

    def island_two(u):
        arrived(16 * PER + 2 * u + 1, hz.at[u])
        cols = pl.ds(128 * u, 128)
        pseudo = (dep[u, 0, 0] + hz[u, 0] + hz[u, 1] + hz[u, 2]) / 8
        momentum = 0.9 * omv[:, cols] + pseudo
        mn_o[:, cols] = momentum
        out = pl.ds(pl.multiple_of(own + u * 128, 128), 128)
        an_o[:, out] = anv[:, out] - 0.7 * (pseudo + 0.9 * momentum)
        for rc, rz in [(0, 2), (1, 2), (0, 1), (1, 1), (0, 3), (1, 3), (1, 0)]:
            send(N_RECV - 1, 12, an_o.at[:, out], an_o.at[:, out], (island(rc, rz), f))

    for s, i in ORDER:
        if s == 6:
            island_one(i)
            continue
        if s == 7:
            island_two(i)
            continue
        r1, r2 = rings(i)
        if s == 0:
            if i // 2 in used:
                u = i // 2
                used.remove(u)
                if len(used) > 1:
                    load_unit(used[1])
                if len(used) == 4:
                    for c in state:
                        c.start()
                pltpu.make_async_copy(og.at[0, :, pl.ds(0, W)], ov.at[u], lsem.at[7 + u]).wait()
            matmul(i)
        if i < 12:
            if s == 0:
                ring_raw(*r1)
            elif s == 1:
                ring_mid(*r1)
            elif s == 2:
                ring_end(*r1)
                ring_raw(*r2)
            elif s == 3:
                ring_mid(*r2)
            elif s == 4:
                ring_end(*r2)
                send(i * PER + 4, 4, T.at[i, 0, 0, 1], LZ.at[i], zz)
            else:
                arrived(i * PER + 4, LZ.at[i])
                add(T.at[i, 0, 0, 0], LZ.at[i])
                finish_chunk(i)
        else:
            if s == 0:
                send(i * PER + 4, 9, T.at[i, :, :, 1], CZ.at[i - 12], zz)
            elif s == 1:
                arrived(i * PER + 4, CZ.at[i - 12])
                for k in range(4):
                    add(T.at[i, k, :, 0], CZ.at[i - 12, k])
                ring_raw(*r1)
            elif s == 2:
                ring_mid(*r1)
            elif s == 3:
                ring_end(*r1)
                ring_raw(*r2)
            elif s == 4:
                ring_mid(*r2)
            else:
                ring_end(*r2)
                finish_chunk(i)

    results = an_o.at[:, pl.ds(0, 7 * 1024)]
    arrived(N_RECV - 1, results)
    for k, whole in enumerate([S1, L1, S2, L2, LZ, CS1, CL1, CS2, CL2, CZ, depc, hz, results]):
        remote(0, k, whole, whole, zz).wait_send()


def hand_on(a, b, c, d, a_o, b_o, c_o, d_o, sem):
    copies = [pltpu.make_async_copy(p, o, sem.at[i]) for i, (p, o) in enumerate([(a, a_o), (b, b_o), (c, c_o), (d, d_o)])]
    for c in copies:
        c.start()
    for c in copies:
        c.wait()


def on_device(*args):
    V = pltpu.VMEM
    anyspace = pl.BlockSpec(memory_space=pl.ANY)
    shapes = tuple(jax.ShapeDtypeStruct(s, F32) for s in [(1, 16, 8192), (1, 16, 8192), (16, 1024), (16, 8192)])
    outs = pl.pallas_call(
        kernel,
        out_shape=tuple(V(s.shape, F32) for s in shapes),
        in_specs=[anyspace] * 8,
        out_specs=[pl.BlockSpec(memory_space=V)] * 4,
        scratch_shapes=[
            V((512, 512), jnp.bfloat16), V((512, 512), jnp.bfloat16), V((8, 512, W), jnp.bfloat16),
            V((16, 8192), F32), V((16, 8192), F32), V((16, 8192), F32), V((16, 8192), F32), V((16, 1024), F32),
            V((512, 512), jnp.bfloat16), V((16, 4, 4, 2, 8, W), F32),
            V((12, 2, 4, 2, 8, W), F32), V((12, 2, 2, 2, 8, W), F32), V((12, 2, 2, 8, W), F32), V((12, 2, 8, W), F32),
            V((12, 8, W), F32),
            V((4, 4, 4, 8, W), F32), V((4, 2, 4, 8, W), F32), V((4, 2, 2, 8, W), F32), V((4, 2, 8, W), F32),
            V((4, 2, 8, W // 2), F32),
            V((8, 2, 4, 16, 128), F32), V((8, 4, 16, 128), F32), V((8, 3, 16, 128), F32),
            pltpu.SemaphoreType.DMA((CLASSES,)), pltpu.SemaphoreType.DMA((N_RECV,)),
            pltpu.SemaphoreType.DMA((15,)),
        ],
        compiler_params=pltpu.CompilerParams(
            collective_id=0, has_side_effects=True, vmem_limit_bytes=58 * 2**20
        ),
        cost_estimate=pl.CostEstimate(flops=4300000000, bytes_accessed=13000000, transcendentals=400000),
        name="round",
    )(*args)
    return pl.pallas_call(
        hand_on,
        out_shape=shapes,
        in_specs=[pl.BlockSpec(memory_space=V)] * 4,
        out_specs=[anyspace] * 4,
        scratch_shapes=[pltpu.SemaphoreType.DMA((4,))],
        name="hand_on",
    )(*[pltpu.with_memory_space_constraint(o, V) for o in outs])


def solution(mesh):
    rows = P("island", "fsdp", None)
    return jax.shard_map(
        on_device,
        mesh=mesh,
        in_specs=(rows,) * 6 + (P("fsdp", None), P("fsdp", "island")),
        out_specs=(rows, rows, P("fsdp", "island"), P("fsdp", None)),
        check_vma=False,
    )
```

time: 120 us -> 110 us (0.917)
  local copies, waits for them, and re-layouts: 7.08 us -> 0 us
  Pallas kernels: 112 us -> 109 us
    unnamed x4 -> x0, local copies, waits for them, and re-layouts: 7.08 us -> none
    pallas_call x1 -> x2, Pallas kernels: 112 us -> 109 us  [the longest x1 108 us: on_device(): pl.pallas_call(kernel, out_shape=tuple((V(s.shape, F32) for s in shapes))...]
where the time goes in v2:
time: 110 us; the launch traced here: 109 us
  Pallas kernels  109 us (99%)
    pallas_call x1, Pallas kernels, on_device(): pl.pallas_call(kernel, out_shape=tuple((V(s.shape, F32) for s in shapes))...  108 us

profile of v2, /device:TPU:1, one launch (start us, length us, event | category | flops | bytes accessed | tf_op | source)
XLA Modules:
  0.0 109.4 jit_solution(7319873412648957888)
XLA Ops:
  0.6 107.6 %round.1 = (f32[1,16,8192]{2,1,0:T(8,128)S(1)}, f32[1,16,8192]{2,1,0:T(8,128)S(1)}, f32[16,1024]{1,0:T(8,128)S(1)}, f32[16,8192]{1,0:T(8,128)S(1)}) custom-call(bf16[1,512,512]{2,1,0:T(8,128)(2,1)} %gate.1, bf16[1,512,512]{2,1,0:T(8,128)(2,1)} %up.1, bf16[1,512,8192]{2,1,0:T(8,128)(2,1)} %og.1, f32[1,16,8192]{2,1,0:T(8,128)} %iw.1, f32[1,16,8192]{2,1,0:T(8,128)} %fm.1, ...), custom_call_target="tpu_custom_call" | custom-call | flops 4300000256 | bytes 13000000 | tf_op jit(solution)/shard_map/round/pallas_call | solution.py:309
  108.2 1.2 %hand_on.1 = (f32[1,16,8192]{2,1,0:T(8,128)}, f32[1,16,8192]{2,1,0:T(8,128)}, f32[16,1024]{1,0:T(8,128)}, f32[16,8192]{1,0:T(8,128)}) custom-call(f32[1,16,8192]{2,1,0:T(8,128)S(1)} %get-tuple-element.8.a, f32[1,16,8192]{2,1,0:T(8,128)S(1)} %get-tuple-element.9.b, f32[16,1024]{1,0:T(8,128)S(1)} %get-tuple-element.10.c, f32[16,8192]{1,0:T(8,128)S(1)} %get-tuple-element.11.d), custom_call_target="tpu_custom_call" | custom-call | tf_op jit(solution)/shard_map/hand_on/pallas_call | solution.py:332

commit v3 on v2

--- a/solution.py
+++ b/solution.py
@@ -12,23 +12,30 @@
 F32 = jnp.float32
 W = 1024
 ORDER = [
-    (0, 0), (0, 6), (0, 1), (0, 7), (1, 0), (1, 6), (0, 2), (0, 8), (0, 12), (1, 1), (1, 7), (2, 0), (0, 14), (2, 6),
-    (0, 3), (1, 2), (1, 8), (1, 12), (2, 1), (3, 6), (2, 7), (3, 0), (0, 13), (1, 3), (0, 9), (2, 8), (3, 1), (4, 0),
-    (2, 2), (1, 9), (1, 14), (2, 12), (4, 6), (4, 1), (3, 7), (3, 2), (0, 15), (2, 3), (2, 9), (0, 4), (3, 8), (2, 14),
-    (0, 10), (3, 12), (4, 7), (4, 2), (0, 5), (3, 9), (3, 3), (5, 0), (1, 13), (5, 6), (0, 11), (5, 1), (3, 14), (1, 4),
-    (1, 10), (6, 0), (4, 8), (4, 12), (4, 3), (1, 5), (1, 11), (4, 9), (1, 15), (5, 7), (2, 13), (5, 2), (4, 14), (5, 8),
-    (6, 3), (5, 3), (7, 0), (2, 10), (5, 9), (5, 12), (2, 4), (6, 1), (6, 4), (2, 11), (7, 3), (2, 15), (2, 5), (3, 13),
-    (7, 1), (5, 14), (3, 4), (7, 4), (3, 10), (3, 11), (3, 15), (3, 5), (4, 10), (4, 13), (4, 11), (4, 15), (4, 4), (4, 5),
-    (5, 10), (5, 13), (5, 11), (5, 15), (5, 4), (5, 5), (6, 6), (6, 5), (6, 7), (6, 2), (7, 6), (7, 5), (7, 7), (7, 2),
+    (0, 2), (0, 8), (0, 15), (0, 9), (0, 3), (0, 0), (1, 2), (0, 13), (1, 8), (0, 11), (1, 3), (1, 9), (1, 15),
+    (1, 0), (0, 12), (2, 8), (1, 11), (2, 2), (2, 3), (2, 9), (1, 13), (2, 15), (2, 0), (3, 8), (0, 14), (0, 7),
+    (3, 9), (0, 5), (2, 11), (2, 13), (3, 2), (3, 3), (4, 8), (0, 10), (4, 9), (3, 15), (0, 1), (3, 0), (1, 5),
+    (1, 12), (1, 7), (3, 11), (3, 13), (4, 2), (4, 15), (4, 3), (0, 6), (0, 4), (1, 1), (1, 10), (1, 14), (5, 8),
+    (4, 0), (5, 9), (5, 2), (5, 3), (6, 0), (2, 5), (6, 1), (5, 0), (2, 7), (6, 2), (4, 13), (2, 12), (6, 9), (4, 11),
+    (5, 15), (1, 6), (7, 0), (6, 6), (1, 4), (5, 11), (7, 1), (7, 2), (7, 9), (6, 8), (2, 10), (8, 0), (2, 14),
+    (2, 1), (3, 7), (7, 6), (3, 5), (5, 13), (8, 9), (3, 12), (7, 8), (6, 4), (2, 6), (2, 4), (3, 10), (3, 14),
+    (3, 1), (8, 8), (4, 7), (7, 4), (3, 6), (4, 12), (5, 5), (3, 4), (4, 14), (5, 10), (6, 14), (5, 7), (4, 6),
+    (5, 12), (6, 7), (5, 1), (6, 12), (5, 14), (5, 4), (6, 3), (6, 10), (5, 6), (6, 5), (6, 13), (7, 14), (6, 11),
+    (7, 7), (7, 12), (7, 3), (7, 10), (7, 5), (7, 13), (8, 14), (7, 11), (8, 7), (8, 12), (8, 3), (8, 10), (8, 5),
+    (8, 13),
 ]
+GROUPS = [(4, None), (1, 0), (1, 1), (6, 0), (6, 1), (7, 0), (7, 1), (5, 0), (5, 1), (0, 0), (0, 1), (3, 0), (3, 1), (2, 0), (2, 1)]
+DIRECT = [2, 4, 11]
+SLANTED = [1, 4, 5, 10]
+GATHER = [1, 6]
 PER = 5
-N_RECV = 16 * PER + 17
-CLASSES = 13
+N_RECV = 16 * PER + 3 * len(GROUPS) + 1
+CLASSES = 16
 
 def kernel(
     gate, up, og, iw, fm, sm, an, om, fn_o, sn_o, mn_o, an_o,
     gv, uv, ov, iwv, fmv, smv, anv, omv,
-    hb, T, L1, S1, L2, S2, LZ, CZ, CL1, CS1, CL2, CS2, dep, depc, hz,
+    hb, T, L1, S1, L2, S2, LZ, CZ, CL1, CS1, CL2, CS2, dep, depc, hz, gz, omr,
     ssem, rsem, lsem,
 ):
     isl = lax.axis_index("island")
@@ -42,6 +49,8 @@
     xp, xm = dev((x + 1) % 4, y, z), dev((x + 3) % 4, y, z)
     yp, ym = dev(x, (y + 1) % 4, z), dev(x, (y + 3) % 4, z)
     zz = dev(x, y, 1 - z)
+    xpz, xmz = dev((x + 1) % 4, y, 1 - z), dev((x + 3) % 4, y, 1 - z)
+    ypz, ymz = dev(x, (y + 1) % 4, 1 - z), dev(x, (y + 3) % 4, 1 - z)
 
     def island(rc, rz):
         return ((zh + rz) % 4) * 2 + (core + rc) % 2
@@ -74,7 +83,12 @@
         for i, (src, dst) in enumerate([(iw.at[0], iwv), (fm.at[0], fmv), (sm.at[0], smv), (an, anv), (om, omv)])
     ]
     barrier = pltpu.get_barrier_semaphore()
-    peers = [xp, xm, yp, ym, zz] + [(island(rc, rz), f) for rc, rz in others]
+    peers = [xp, xm, yp, ym, zz]
+    if any(c < 6 for c in SLANTED):
+        peers += [ypz, ymz]
+    if any(6 <= c < 12 for c in SLANTED):
+        peers += [xpz, xmz]
+    peers += [(island(rc, rz), f) for rc, rz in others]
     for d in peers:
         pl.semaphore_signal(barrier, inc=1, device_id=d, device_id_type=MESH)
 
@@ -127,20 +141,20 @@
 
         lax.fori_loop(0, W // 256, body, 0)
 
-    def ring_raw(n, k, blk, one, two, ones, twos, plus, minus):
+    def ring_raw(n, k, blk, one, two, ones, twos, plus, minus, plus1, minus1):
         send(n, k, blk(2, 0), one(0), plus)
         send(n, k, blk(2, 1), one(1), minus)
-        send(n + 1, k + 1, blk(1, 1), two(0, 1), plus)
+        send(n + 1, k + 1, blk(1, 1), two(0, 1), plus1)
         send(n + 1, k + 1, blk(3, 0), two(1, 0), minus)
 
-    def ring_mid(n, k, blk, one, two, ones, twos, plus, minus):
+    def ring_mid(n, k, blk, one, two, ones, twos, plus, minus, plus1, minus1):
         arrived(n, ones)
         add(blk(1, 0), one(0))
         send(n + 1, k + 1, blk(1, 0), two(0, 0), plus)
         add(blk(3, 1), one(1))
-        send(n + 1, k + 1, blk(3, 1), two(1, 1), minus)
-
-    def ring_end(n, k, blk, one, two, ones, twos, plus, minus):
+        send(n + 1, k + 1, blk(3, 1), two(1, 1), minus1)
+
+    def ring_end(n, k, blk, one, two, ones, twos, plus, minus, plus1, minus1):
         arrived(n + 1, twos)
         add(blk(0), two(0), two(1))
 
@@ -176,7 +190,10 @@
         along_x, along_y = (xp, xm), (yp, ym)
         d1, d2 = (along_x, along_y) if c < 6 or 12 <= c < 14 else (along_y, along_x)
         n = c * PER
-        return (n, k, b1, s1, l1) + w1 + d1, (n + 2, k + 2, b2, s2, l2) + w2 + d2
+        e2 = d2
+        if c in SLANTED:
+            e2 = (ypz, ymz) if c < 6 else (xpz, xmz)
+        return (n, k, b1, s1, l1) + w1 + d1 + d1, (n + 2, k + 2, b2, s2, l2) + w2 + d2 + e2
 
     def update(c):
         u, h = c // 2, c % 2
@@ -207,31 +224,81 @@
         if updated[0] == 0:
             for s in state:
                 s.wait()
+            for k, g in enumerate(GATHER):
+                u, rows, n = group(g)
+                for rz in (2, 1, 3):
+                    send(n + 2, 14, omv.at[rows, pl.ds(128 * u, 128)], omr.at[k, rz - 1], (island(0, rz), f))
         update(c)
         updated[0] += 1
-        done[c] = True
-        if done.get(c ^ 1):
-            send(16 * PER + 2 * u, 10, dep.at[u, 1], depc.at[u], (island(1, 0), f))
-
-    done = {}
+        done.add(c)
+        for g, (u, h) in enumerate(GROUPS):
+            if c // 2 == u and (h == c % 2 or h is None and c ^ 1 in done):
+                u, rows, n = group(g)
+                send(n, 10, dep.at[u, 1, :, rows], depc.at[u, :, rows], (island(1, 0), f))
+
+    done = set()
     own = isl * 1024
 
-    def island_one(u):
-        arrived(16 * PER + 2 * u, depc.at[u])
-        add(dep.at[u, 0], depc.at[u])
+    def group(g):
+        u, h = GROUPS[g]
+        return u, pl.ds(0, 16) if h is None else pl.ds(8 * h, 8), 16 * PER + 3 * g
+
+    def island_one(g):
+        u, rows, n = group(g)
+        arrived(n, depc.at[u, :, rows])
+        add(dep.at[u, 0, :, rows], depc.at[u, :, rows])
+        if g in GATHER:
+            for rz in (2, 1, 3):
+                send(n + 1, 13, dep.at[u, 0, :, rows], gz.at[GATHER.index(g), rz - 1], (island(0, rz), f))
+            return
         for rz in (2, 1, 3):
-            send(16 * PER + 2 * u + 1, 11, dep.at[u, 0, rz], hz.at[u, rz - 1], (island(0, rz), f))
-
-    def island_two(u):
-        arrived(16 * PER + 2 * u + 1, hz.at[u])
+            send(n + 1, 11, dep.at[u, 0, rz, rows], hz.at[u, rz - 1, rows], (island(0, rz), f))
+
+    def gathered(g):
+        u, rows, n = group(g)
+        k = GATHER.index(g)
+        arrived(n + 2, omr.at[k])
+        arrived(n + 1, gz.at[k])
+
+        def result(r, old):
+            pseudo = ((dep[u, 0, r, rows] + gz[k, 1, (r + 2) % 4]) + (gz[k, 0, (r + 1) % 4] + gz[k, 2, (r + 3) % 4])) / 8
+            momentum = 0.9 * old + pseudo
+            out = pl.ds(pl.multiple_of(island(0, r) * 1024 + u * 128, 128), 128)
+            an_o[rows, out] = anv[rows, out] - 0.7 * (pseudo + 0.9 * momentum)
+            send(N_RECV - 1, 15, an_o.at[rows, out], an_o.at[rows, out], (island(1, 0), f))
+            return momentum
+
         cols = pl.ds(128 * u, 128)
-        pseudo = (dep[u, 0, 0] + hz[u, 0] + hz[u, 1] + hz[u, 2]) / 8
-        momentum = 0.9 * omv[:, cols] + pseudo
-        mn_o[:, cols] = momentum
+        mn_o[rows, cols] = result(0, omv[rows, cols])
+        for r in (1, 2, 3):
+            result(r, omr[k, 3 - r])
+
+    def island_two(g):
+        if g in GATHER:
+            gathered(g)
+            return
+        u, rows, n = group(g)
+        arrived(n + 1, hz.at[u, :, rows])
+        cols = pl.ds(128 * u, 128)
+        pseudo = (dep[u, 0, 0, rows] + hz[u, 0, rows] + hz[u, 1, rows] + hz[u, 2, rows]) / 8
+        momentum = 0.9 * omv[rows, cols] + pseudo
+        mn_o[rows, cols] = momentum
         out = pl.ds(pl.multiple_of(own + u * 128, 128), 128)
-        an_o[:, out] = anv[:, out] - 0.7 * (pseudo + 0.9 * momentum)
-        for rc, rz in [(0, 2), (1, 2), (0, 1), (1, 1), (0, 3), (1, 3), (1, 0)]:
-            send(N_RECV - 1, 12, an_o.at[:, out], an_o.at[:, out], (island(rc, rz), f))
+        an_o[rows, out] = anv[rows, out] - 0.7 * (pseudo + 0.9 * momentum)
+        res = an_o.at[rows, out]
+        for rz in (2, 1, 3):
+            send(n + 2, 12, res, res, (island(0, rz), f))
+            if g in DIRECT:
+                send(N_RECV - 1, 12, res, res, (island(1, rz), f))
+        send(N_RECV - 1, 12, res, res, (island(1, 0), f))
+
+    def island_three(g):
+        u, rows, n = group(g)
+        arrived(n + 2, an_o.at[rows, pl.ds(0, 3 * 128)])
+        if g not in DIRECT:
+            for rz in (1, 2, 3):
+                out = pl.ds(pl.multiple_of(island(0, rz) * 1024 + u * 128, 128), 128)
+                send(N_RECV - 1, 12, an_o.at[rows, out], an_o.at[rows, out], (island(1, 0), f))
 
     for s, i in ORDER:
         if s == 6:
@@ -239,6 +306,9 @@
             continue
         if s == 7:
             island_two(i)
+            continue
+        if s == 8:
+            island_three(i)
             continue
         r1, r2 = rings(i)
         if s == 0:
@@ -260,6 +330,8 @@
             elif s == 2:
                 ring_end(*r1)
                 ring_raw(*r2)
+                if i in SLANTED:
+                    send(i * PER + 4, 4, T.at[i, 0, 0, 1], LZ.at[i], zz)
             elif s == 3:
                 ring_mid(*r2)
             elif s == 4:
@@ -267,7 +339,11 @@
                 send(i * PER + 4, 4, T.at[i, 0, 0, 1], LZ.at[i], zz)
             else:
                 arrived(i * PER + 4, LZ.at[i])
-                add(T.at[i, 0, 0, 0], LZ.at[i])
+                more = []
+                if i in SLANTED:
+                    arrived(i * PER + 3, L2.at[i])
+                    more = [L2.at[i, d, k] for d in (0, 1) for k in (0, 1)]
+                add(T.at[i, 0, 0, 0], LZ.at[i], *more)
                 finish_chunk(i)
         else:
             if s == 0:
@@ -288,10 +364,18 @@
                 ring_end(*r2)
                 finish_chunk(i)
 
-    results = an_o.at[:, pl.ds(0, 7 * 1024)]
-    arrived(N_RECV - 1, results)
-    for k, whole in enumerate([S1, L1, S2, L2, LZ, CS1, CL1, CS2, CL2, CZ, depc, hz, results]):
+    for g in DIRECT:
+        island_three(g)
+    arrived(N_RECV - 1, an_o.at[:, pl.ds(0, 4 * 1024)])
+    plain = 16 - len(GATHER)
+    for k, whole in [
+        (0, S1), (1, L1), (2, S2), (3, L2), (4, LZ), (5, CS1), (6, CL1), (7, CS2), (8, CL2), (9, CZ), (10, depc),
+        (11, hz.at[pl.ds(0, plain // 2)]), (12, an_o.at[:, pl.ds(0, 7 * plain // 2 * 128)]),
+    ]:
         remote(0, k, whole, whole, zz).wait_send()
+    if GATHER:
+        for k, whole in [(13, gz), (14, omr), (15, an_o.at[:, pl.ds(0, 2 * len(GATHER) * 128)])]:
+            remote(0, k, whole, whole, zz).wait_send()
 
 
 def hand_on(a, b, c, d, a_o, b_o, c_o, d_o, sem):
@@ -320,6 +404,7 @@
             V((4, 4, 4, 8, W), F32), V((4, 2, 4, 8, W), F32), V((4, 2, 2, 8, W), F32), V((4, 2, 8, W), F32),
             V((4, 2, 8, W // 2), F32),
             V((8, 2, 4, 16, 128), F32), V((8, 4, 16, 128), F32), V((8, 3, 16, 128), F32),
+            V((max(len(GATHER), 1), 3, 4, 8, 128), F32), V((max(len(GATHER), 1), 3, 8, 128), F32),
             pltpu.SemaphoreType.DMA((CLASSES,)), pltpu.SemaphoreType.DMA((N_RECV,)),
             pltpu.SemaphoreType.DMA((15,)),
         ],

time: 110 us -> 107 us (0.973)
  Pallas kernels: 109 us -> 106 us
    pallas_call x1, Pallas kernels: 108 us -> 105 us  [on_device(): pl.pallas_call(kernel, out_shape=tuple((V(s.shape, F32) for s in shapes))...]
where the time goes in v3:
time: 107 us
  Pallas kernels  106 us (99%)
    pallas_call x1, Pallas kernels, on_device(): pl.pallas_call(kernel, out_shape=tuple((V(s.shape, F32) for s in shapes))...  105 us

profile of v3, /device:TPU:1, one launch (start us, length us, event | category | flops | bytes accessed | tf_op | source)
XLA Modules:
  0.0 106.9 jit_solution(9098783275538449861)
XLA Ops:
  0.6 105.1 %round.1 = (f32[1,16,8192]{2,1,0:T(8,128)S(1)}, f32[1,16,8192]{2,1,0:T(8,128)S(1)}, f32[16,1024]{1,0:T(8,128)S(1)}, f32[16,8192]{1,0:T(8,128)S(1)}) custom-call(bf16[1,512,512]{2,1,0:T(8,128)(2,1)} %gate.1, bf16[1,512,512]{2,1,0:T(8,128)(2,1)} %up.1, bf16[1,512,8192]{2,1,0:T(8,128)(2,1)} %og.1, f32[1,16,8192]{2,1,0:T(8,128)} %iw.1, f32[1,16,8192]{2,1,0:T(8,128)} %fm.1, ...), custom_call_target="tpu_custom_call" | custom-call | flops 4300000256 | bytes 13000000 | tf_op jit(solution)/shard_map/round/pallas_call | solution.py:393
  105.7 1.2 %hand_on.1 = (f32[1,16,8192]{2,1,0:T(8,128)}, f32[1,16,8192]{2,1,0:T(8,128)}, f32[16,1024]{1,0:T(8,128)}, f32[16,8192]{1,0:T(8,128)}) custom-call(f32[1,16,8192]{2,1,0:T(8,128)S(1)} %get-tuple-element.8.a, f32[1,16,8192]{2,1,0:T(8,128)S(1)} %get-tuple-element.9.b, f32[16,1024]{1,0:T(8,128)S(1)} %get-tuple-element.10.c, f32[16,8192]{1,0:T(8,128)S(1)} %get-tuple-element.11.d), custom_call_target="tpu_custom_call" | custom-call | tf_op jit(solution)/shard_map/hand_on/pallas_call | solution.py:417

commit v4 on v3

--- a/solution.py
+++ b/solution.py
@@ -141,11 +141,38 @@
 
         lax.fori_loop(0, W // 256, body, 0)
 
-    def ring_raw(n, k, blk, one, two, ones, twos, plus, minus, plus1, minus1):
+    def blocks(c, ks):
+        u, h = c // 2, c % 2
+        if c < 6:
+            parts = [hb[256 * h + 64 * k : 256 * h + 64 * k + 64, :] for k in ks]
+        else:
+            parts = [hb[256 * h + 64 * a + 16 * k : 256 * h + 64 * a + 16 * k + 16, :] for k in ks for a in range(4)]
+        left = jnp.concatenate(parts, axis=0)
+
+        def body(t, _):
+            cols = pl.ds(pl.multiple_of(t * 256, 256), 256)
+            r = lax.dot_general(left, ov[u, :, cols], (((1,), (0,)), ((), ())), preferred_element_type=F32)
+            r = r.astype(jnp.bfloat16).astype(F32).reshape(len(ks), 4, 2, 8, 256)
+            for n, k in enumerate(ks):
+                if c < 6:
+                    T[c, k, :, :, :, cols] = r[n]
+                else:
+                    T[c, :, k, :, :, cols] = r[n]
+            return 0
+
+        lax.fori_loop(0, W // 256, body, 0)
+
+    def ring_far(n, k, blk, one, two, ones, twos, plus, minus, plus1, minus1):
         send(n, k, blk(2, 0), one(0), plus)
         send(n, k, blk(2, 1), one(1), minus)
+
+    def ring_near(n, k, blk, one, two, ones, twos, plus, minus, plus1, minus1):
         send(n + 1, k + 1, blk(1, 1), two(0, 1), plus1)
         send(n + 1, k + 1, blk(3, 0), two(1, 0), minus)
+
+    def ring_raw(*ring):
+        ring_far(*ring)
+        ring_near(*ring)
 
     def ring_mid(n, k, blk, one, two, ones, twos, plus, minus, plus1, minus1):
         arrived(n, ones)
@@ -215,7 +242,7 @@
             dep[u, rc, rz, rows, :] = anv[rows, cols] - (w - 0.05 * (upd + 0.4 * w))
             return 0
 
-        lax.fori_loop(0, 8, body, 0)
+        lax.fori_loop(0, 8, body, 0, unroll=True)
 
     updated = [0]
 
@@ -300,6 +327,19 @@
                 out = pl.ds(pl.multiple_of(island(0, rz) * 1024 + u * 128, 128), 128)
                 send(N_RECV - 1, 12, an_o.at[rows, out], an_o.at[rows, out], (island(1, 0), f))
 
+    def fetched(u):
+        used.remove(u)
+        if len(used) > 1:
+            load_unit(used[1])
+        if len(used) == 4:
+            for c in state:
+                c.start()
+        pltpu.make_async_copy(og.at[0, :, pl.ds(0, W)], ov.at[u], lsem.at[7 + u]).wait()
+
+    early = [i for s, i in ORDER if s == 0][:2]
+    if max(early) >= 12 or early[0] // 2 == early[1] // 2:
+        early = []
+
     for s, i in ORDER:
         if s == 6:
             island_one(i)
@@ -311,16 +351,19 @@
             island_three(i)
             continue
         r1, r2 = rings(i)
+        if s == 0 and i in early:
+            if i == early[0]:
+                for c in early:
+                    fetched(c // 2)
+                    blocks(c, [2])
+                    ring_far(*rings(c)[0])
+                for c in early:
+                    blocks(c, [1, 3, 0])
+                    ring_near(*rings(c)[0])
+            continue
         if s == 0:
             if i // 2 in used:
-                u = i // 2
-                used.remove(u)
-                if len(used) > 1:
-                    load_unit(used[1])
-                if len(used) == 4:
-                    for c in state:
-                        c.start()
-                pltpu.make_async_copy(og.at[0, :, pl.ds(0, W)], ov.at[u], lsem.at[7 + u]).wait()
+                fetched(i // 2)
             matmul(i)
         if i < 12:
             if s == 0:

time: 107 us -> 107 us (level)
  no operation moved by 1% of the time
where the time goes in v4:
time: 107 us; the launch traced here: 106 us
  Pallas kernels  106 us (99%)
    pallas_call x1, Pallas kernels, on_device(): pl.pallas_call(kernel, out_shape=tuple((V(s.shape, F32) for s in shapes))...  105 us

profile of v4, /device:TPU:1, one launch (start us, length us, event | category | flops | bytes accessed | tf_op | source)
XLA Modules:
  0.0 106.4 jit_solution(6255187252358508248)
XLA Ops:
  0.6 104.6 %round.1 = (f32[1,16,8192]{2,1,0:T(8,128)S(1)}, f32[1,16,8192]{2,1,0:T(8,128)S(1)}, f32[16,1024]{1,0:T(8,128)S(1)}, f32[16,8192]{1,0:T(8,128)S(1)}) custom-call(bf16[1,512,512]{2,1,0:T(8,128)(2,1)} %gate.1, bf16[1,512,512]{2,1,0:T(8,128)(2,1)} %up.1, bf16[1,512,8192]{2,1,0:T(8,128)(2,1)} %og.1, f32[1,16,8192]{2,1,0:T(8,128)} %iw.1, f32[1,16,8192]{2,1,0:T(8,128)} %fm.1, ...), custom_call_target="tpu_custom_call" | custom-call | flops 4300000256 | bytes 13000000 | tf_op jit(solution)/shard_map/round/pallas_call | solution.py:436
  105.2 1.2 %hand_on.1 = (f32[1,16,8192]{2,1,0:T(8,128)}, f32[1,16,8192]{2,1,0:T(8,128)}, f32[16,1024]{1,0:T(8,128)}, f32[16,8192]{1,0:T(8,128)}) custom-call(f32[1,16,8192]{2,1,0:T(8,128)S(1)} %get-tuple-element.8.a, f32[1,16,8192]{2,1,0:T(8,128)S(1)} %get-tuple-element.9.b, f32[16,1024]{1,0:T(8,128)S(1)} %get-tuple-element.10.c, f32[16,8192]{1,0:T(8,128)S(1)} %get-tuple-element.11.d), custom_call_target="tpu_custom_call" | custom-call | tf_op jit(solution)/shard_map/hand_on/pallas_call | solution.py:460
